TPU v7x, 32 devices: a whole 2x2x4 slice. The times are simulated.
32 devices in a mesh: groups: 2 (over x), rows: 16 (over z, y, core).
Axes of the slice: x: 2, y: 2, z: 4, core: 2. Of those that a mesh axis runs over, the one named last changes fastest.
Arguments:
- orbitals: float32 [32768, 1024], P('rows', 'groups'), parts along dimension 1, may hold values from -6 to 6
- trial_orbitals: float32 [32768, 1024], P('rows', 'groups'), parts along dimension 1, may hold values from -0.03125 to 0.03125
- angles: float32 [128], replicated, may hold values from -3.140625 to 3.140625
- horizontal_index: int32 [4, 64, 512], P('groups', 'rows'), parts along dimension 0, may hold values from 0 to 127
- horizontal_mask: int32 [4, 64, 512], P('groups', 'rows'), parts along dimension 0, may hold values 0 or 1
- vertical_index: int32 [8, 64, 512], P('groups', 'rows'), parts along dimension 0, may hold values from 0 to 127
- vertical_mask: int32 [8, 64, 512], P('groups', 'rows'), parts along dimension 0, may hold values 0 or 1
Outputs:
- evolved: float32 [32768, 1024], P('rows', 'groups'), parts along dimension 1
- intersection: float32 [1024, 512], P('groups'), parts along dimension 0
There are 2 independent parts, one for each index of `groups`. A program takes and returns all parts, laid end to end along the dimension named above; an argument that names none is the same for every part. Nothing has to cross between parts.
All inputs are finite; a program needn't handle non-finite values. No bound on the sum of `horizontal_mask` or of `vertical_mask` on one device may be relied on, other than what follows from the above.
Results may differ from a plain program's by a relative error of at most 0.00012.
Values sent between devices are 32-bit elements; how exact they have to be, the bound alone decides.
A program may use at most 128 MiB of HBM per device.

v0:
```python
import functools

import jax
import jax.numpy as jnp
from jax import lax
from jax.experimental import pallas as pl
from jax.experimental.pallas import tpu as pltpu
from jax.sharding import PartitionSpec as P

LANES = 128
BLOCK = 64


def coefficient_kernel(layers_across, layers_up, rows, code_ref, cos_ref, sin_ref, coef_ref, edge_ref):
    count, width = code_ref.shape
    blocks = width // LANES
    cosines, sines = [], []
    for block in range(blocks):
        code = code_ref[:, block * LANES : (block + 1) * LANES]
        place = jnp.maximum(code, 0)
        table_cos = jnp.broadcast_to(cos_ref[...], code.shape)
        table_sin = jnp.broadcast_to(sin_ref[...], code.shape)
        picked_cos = jnp.take_along_axis(table_cos, place, axis=1, mode="promise_in_bounds")
        picked_sin = jnp.take_along_axis(table_sin, place, axis=1, mode="promise_in_bounds")
        cosines.append(jnp.where(code >= 0, picked_cos, 1.0))
        sines.append(jnp.where(code >= 0, picked_sin, 0.0))
    backward = LANES - 1 - lax.broadcasted_iota(jnp.int32, (count, LANES), 1)

    def reverse(parts):
        return [jnp.take_along_axis(part, backward, axis=1, mode="promise_in_bounds") for part in parts[::-1]]

    reverse_cos = jnp.concatenate(reverse(cosines), axis=1)
    reverse_sin = jnp.concatenate(reverse(sines), axis=1)
    cosine = jnp.concatenate(cosines, axis=1)
    sine = jnp.concatenate(sines, axis=1)
    position = lax.broadcasted_iota(jnp.int32, (count, width), 1)
    last_cos = pltpu.roll(cosine, 1, 1)
    last_sin = pltpu.roll(sine, 1, 1)
    diagonals, neighbours = [], []
    for layer in range(layers_across):
        first = position % 2 == layer % 2
        diagonal = jnp.where(first, cosine, last_cos)
        neighbour = jnp.where(first, -sine, last_sin)
        if layer % 2:
            inside = (position > 0) & (position < width - 1)
            diagonal = jnp.where(inside, diagonal, 1.0)
            neighbour = jnp.where(inside, neighbour, 0.0)
        diagonals.append(diagonal)
        neighbours.append(neighbour)
    lanes = coef_ref.shape[2]
    for row in range(rows):
        lines = []
        for layer in range(layers_across):
            at = layer * rows + row
            lines += [diagonals[layer][at : at + 1], neighbours[layer][at : at + 1]]
        for layer in range(layers_up):
            at = (layers_across + layer) * rows + row
            from_cos, from_sin = (reverse_cos, reverse_sin) if row % 2 else (cosine, sine)
            lines += [from_cos[at : at + 1], from_sin[at : at + 1]]
        lines.append(jnp.zeros((lanes - len(lines), width), jnp.float32))
        coef_ref[row] = jnp.transpose(jnp.concatenate(lines, axis=0))
    edges = []
    for layer in range(1, layers_up, 2):
        at = (layers_across + layer) * rows + rows - 1
        edges += [reverse_cos[at : at + 1], reverse_sin[at : at + 1]]
    spare = edge_ref.shape[0] - len(edges)
    if spare:
        edges.append(jnp.zeros((spare, width), jnp.float32))
    edge_ref[...] = jnp.concatenate(edges, axis=0)


def flip(block):
    size, columns = block.shape
    view = block.reshape(size // 8, 8, columns)
    place = lax.broadcasted_iota(jnp.int32, view.shape, 1)
    view = jnp.where(place % 2 == 0, pltpu.roll(view, 7, 1), pltpu.roll(view, 1, 1))
    view = jnp.where(place % 4 < 2, pltpu.roll(view, 6, 1), pltpu.roll(view, 2, 1))
    view = pltpu.roll(view, 4, 1)
    view = jnp.concatenate([view[k : k + 1] for k in range(size // 8)][::-1], axis=0)
    return view.reshape(size, columns)


def split(value):
    high = value.astype(jnp.bfloat16)
    low = (value - high.astype(jnp.float32)).astype(jnp.bfloat16)
    return high, low


def step_kernel(
    devices,
    layers_across,
    layers_up,
    orbital_ref,
    trial_ref,
    coef_ref,
    edge_ref,
    evolved_ref,
    partial_ref,
    state,
    from_last,
    from_next,
    edge_in,
    edge_coef,
    turned,
    trial_high,
    trial_low,
    send_sem,
    recv_sem,
    edge_sem,
):
    rows, width = coef_ref.shape[0], coef_ref.shape[1]
    chunks = state.shape[0]
    steps = width // BLOCK
    stages = layers_up // 2
    me = lax.axis_index("rows")
    after = lax.rem(me + 1, devices)
    before = lax.rem(me + devices - 1, devices)

    barrier = pltpu.get_barrier_semaphore()
    for neighbour in (before, after):
        pl.semaphore_signal(barrier, inc=1, device_id={"rows": neighbour}, device_id_type=pl.DeviceIdType.MESH)
    pl.semaphore_wait(barrier, 2)

    edge_copy = pltpu.make_async_remote_copy(
        src_ref=edge_ref,
        dst_ref=edge_in,
        send_sem=edge_sem.at[0],
        recv_sem=edge_sem.at[1],
        device_id={"rows": after},
        device_id_type=pl.DeviceIdType.MESH,
    )
    edge_copy.start()

    def exchange(stage, chunk):
        down = pltpu.make_async_remote_copy(
            src_ref=state.at[chunk, 0],
            dst_ref=from_next.at[stage, chunk],
            send_sem=send_sem.at[stage, 0, chunk],
            recv_sem=recv_sem.at[stage, 0, chunk],
            device_id={"rows": before},
            device_id_type=pl.DeviceIdType.MESH,
        )
        up = pltpu.make_async_remote_copy(
            src_ref=state.at[chunk, rows - 1],
            dst_ref=from_last.at[stage, chunk],
            send_sem=send_sem.at[stage, 1, chunk],
            recv_sem=recv_sem.at[stage, 1, chunk],
            device_id={"rows": after},
            device_id_type=pl.DeviceIdType.MESH,
        )
        return down, up

    def columns_of(chunk):
        return pl.ds(pl.multiple_of(chunk * LANES, LANES), LANES)

    def vertical(row, layer, place):
        lane = 2 * (layers_across + layer)
        pair = coef_ref[row, place, :]
        return pair[:, lane : lane + 1], pair[:, lane + 1 : lane + 2]

    def open_chunk(chunk, carry):
        columns = columns_of(chunk)
        position = lax.broadcasted_iota(jnp.int32, (width, LANES), 0)
        for row in range(rows):
            value = orbital_ref[pl.ds(row * width, width), columns]
            for layer in range(layers_across):
                diagonal = coef_ref[row, :, 2 * layer : 2 * layer + 1]
                beside = coef_ref[row, :, 2 * layer + 1 : 2 * layer + 2]
                partner = jnp.where(
                    position % 2 == layer % 2, pltpu.roll(value, width - 1, 0), pltpu.roll(value, 1, 0)
                )
                value = diagonal * value + beside * partner
            turned[row] = value

        def pairs(step, carry):
            start = pl.multiple_of(step * BLOCK, BLOCK)
            mirrored = pl.multiple_of(width - BLOCK - step * BLOCK, BLOCK)
            place = pl.ds(start, BLOCK)
            for row in range(0, rows, 2):
                lower = turned[row, place, :]
                upper = flip(turned[row + 1, pl.ds(mirrored, BLOCK), :])
                cosine, sine = vertical(row, 0, place)
                state[chunk, row, place, :] = cosine * lower - sine * upper
                state[chunk, row + 1, place, :] = sine * lower + cosine * upper
            return carry

        lax.fori_loop(0, steps, pairs, 0)
        for copy in exchange(0, chunk):
            copy.start()
        return carry

    lax.fori_loop(0, chunks, open_chunk, 0)

    for row in range(rows):
        place = pl.ds(row * width, width)

        def turn(part, carry):
            columns = columns_of(part)
            high, low = split(jnp.transpose(trial_ref[place, columns]))
            trial_high[columns, place] = high
            trial_low[columns, place] = low
            return carry

        lax.fori_loop(0, trial_ref.shape[1] // LANES, turn, 0)

    edge_copy.wait()
    edge_coef[...] = jnp.transpose(edge_in[...])

    def crossing(stage, chunk, place):
        layer = 2 * stage + 1
        values = [state[chunk, row, place, :] for row in range(rows)]
        edge = edge_coef[place, :]
        edge_cos = edge[:, 2 * stage : 2 * stage + 1]
        edge_sin = edge[:, 2 * stage + 1 : 2 * stage + 2]
        new = list(values)
        new[0] = edge_sin * from_last[stage, chunk, place, :] + edge_cos * values[0]
        for row in range(1, rows - 1, 2):
            cosine, sine = vertical(row, layer, place)
            new[row] = cosine * values[row] - sine * values[row + 1]
            new[row + 1] = sine * values[row] + cosine * values[row + 1]
        cosine, sine = vertical(rows - 1, layer, place)
        new[rows - 1] = cosine * values[rows - 1] - sine * from_next[stage, chunk, place, :]
        return new

    for stage in range(stages):
        final = stage == stages - 1

        def advance(chunk, carry):
            for copy in exchange(stage, chunk):
                copy.wait()

            def middle(step, carry):
                place = pl.ds(pl.multiple_of(step * BLOCK, BLOCK), BLOCK)
                new = crossing(stage, chunk, place)
                for row in range(0, rows, 2):
                    cosine, sine = vertical(row, 2 * stage + 2, place)
                    state[chunk, row, place, :] = cosine * new[row] - sine * new[row + 1]
                    state[chunk, row + 1, place, :] = sine * new[row] + cosine * new[row + 1]
                return carry

            def close(step, carry):
                start = step * BLOCK
                place = pl.ds(pl.multiple_of(start, BLOCK), BLOCK)
                new = crossing(stage, chunk, place)
                for row in range(rows):
                    if row % 2:
                        at = pl.ds(pl.multiple_of((row + 1) * width - BLOCK - start, BLOCK), BLOCK)
                        evolved_ref[at, columns_of(chunk)] = flip(new[row])
                    else:
                        at = pl.ds(pl.multiple_of(row * width + start, BLOCK), BLOCK)
                        evolved_ref[at, columns_of(chunk)] = new[row]
                return carry

            lax.fori_loop(0, steps, close if final else middle, 0)
            if not final:
                for copy in exchange(stage + 1, chunk):
                    copy.start()
                return carry
            total = jnp.zeros((partial_ref.shape[0], LANES), jnp.float32)
            for row in range(rows):
                place = pl.ds(row * width, width)
                high, low = split(evolved_ref[place, columns_of(chunk)])
                total += jnp.dot(trial_high[:, place], high, preferred_element_type=jnp.float32)
                total += jnp.dot(trial_high[:, place], low, preferred_element_type=jnp.float32)
                total += jnp.dot(trial_low[:, place], high, preferred_element_type=jnp.float32)
            partial_ref[:, columns_of(chunk)] = total
            return carry

        lax.fori_loop(0, chunks, advance, 0)


def per_device(
    orbitals,
    trial_orbitals,
    angles,
    horizontal_index,
    horizontal_mask,
    vertical_index,
    vertical_mask,
):
    devices = lax.axis_size("rows")
    layers_across, rows, width = horizontal_index.shape
    layers_up = vertical_index.shape[0]
    modes, columns = orbitals.shape
    trials = trial_orbitals.shape[1]
    chunks = columns // LANES
    stages = layers_up // 2
    code = jnp.concatenate(
        [
            jnp.where(horizontal_mask == 1, horizontal_index, -1).reshape(layers_across * rows, width),
            jnp.where(vertical_mask == 1, vertical_index, -1).reshape(layers_up * rows, width),
        ],
        axis=0,
    )
    lanes = -(-2 * (layers_across + layers_up) // 8) * 8
    edges = -(-2 * stages // 8) * 8
    coef, edge = pl.pallas_call(
        functools.partial(coefficient_kernel, layers_across, layers_up, rows),
        out_shape=(
            jax.ShapeDtypeStruct((rows, width, lanes), jnp.float32),
            jax.ShapeDtypeStruct((edges, width), jnp.float32),
        ),
        name="coefficients",
    )(code, jnp.cos(angles)[None, :], jnp.sin(angles)[None, :])

    in_vmem = pl.BlockSpec(memory_space=pltpu.VMEM)
    evolved, partial_value = pl.pallas_call(
        functools.partial(step_kernel, devices, layers_across, layers_up),
        out_shape=(
            jax.ShapeDtypeStruct((modes, columns), jnp.float32),
            jax.ShapeDtypeStruct((trials, columns), jnp.float32),
        ),
        in_specs=[in_vmem] * 4,
        out_specs=(in_vmem, in_vmem),
        scratch_shapes=[
            pltpu.VMEM((chunks, rows, width, LANES), jnp.float32),
            pltpu.VMEM((stages, chunks, width, LANES), jnp.float32),
            pltpu.VMEM((stages, chunks, width, LANES), jnp.float32),
            pltpu.VMEM((edges, width), jnp.float32),
            pltpu.VMEM((width, edges), jnp.float32),
            pltpu.VMEM((rows, width, LANES), jnp.float32),
            pltpu.VMEM((trials, modes), jnp.bfloat16),
            pltpu.VMEM((trials, modes), jnp.bfloat16),
            pltpu.SemaphoreType.DMA((stages, 2, chunks)),
            pltpu.SemaphoreType.DMA((stages, 2, chunks)),
            pltpu.SemaphoreType.DMA((2,)),
        ],
        compiler_params=pltpu.CompilerParams(
            collective_id=0, has_side_effects=True, vmem_limit_bytes=50 * 1024 * 1024
        ),
        name="trotter_step",
    )(orbitals, trial_orbitals, coef, edge)
    return evolved, lax.psum(partial_value, "rows")


def solution(mesh):
    in_specs = (
        P("rows", "groups"),
        P("rows", "groups"),
        P(),
        P("groups", "rows", None),
        P("groups", "rows", None),
        P("groups", "rows", None),
        P("groups", "rows", None),
    )
    out_specs = (P("rows", "groups"), P("groups", None))
    return jax.shard_map(
        per_device, mesh=mesh, in_specs=in_specs, out_specs=out_specs, check_vma=False
    )
```

profile of v0, /device:TPU:0, one launch (start us, length us, event | category | flops | bytes accessed | tf_op | source)
XLA Modules:
  0.0 181.9 jit_solution(16337634011324716334)
XLA Ops:
  7.2 0.0 all-reduce.2.cloned.1.call-start
  7.2 1.3 sine_bitcast_fusion
  8.5 0.7 compare_select_fusion.1
  9.2 0.8 compare_select_fusion
  10.1 0.6 pad_add_fusion.code_ref
  10.7 2.3 %coefficients.1 = (f32[4,512,16]{2,1,0:T(8,128)}, f32[8,512]{1,0:T(8,128)}) custom-call(s32[24,512]{1,0:T(8,128)} %pad_add_fusion.code_ref, f32[1,128]{1,0:T(1,128)} %get-tuple-element.11.cos_ref, f32[1,128]{1,0:T(1,128)} %get-tuple-element.10.sin_ref), custom_call_target="tpu_custom_call" | custom-call | tf_op jit(solution)/shard_map/coefficients/pallas_call | solution.py:297
  13.0 0.0 copy-start
  13.0 1.2 copy-done
  14.3 0.0 copy-start.1
  14.3 0.7 copy-done.1
  15.0 50.9 %trotter_step.1 = (f32[2048,512]{1,0:T(8,128)}, f32[512,512]{1,0:T(8,128)}) custom-call(f32[2048,512]{1,0:T(8,128)} %orbital_ref.1, f32[2048,512]{1,0:T(8,128)} %trial_ref.1, f32[4,512,16]{2,1,0:T(8,128)S(1)} %copy-done, f32[8,512]{1,0:T(8,128)S(1)} %copy-done.1), custom_call_target="tpu_custom_call" | custom-call | tf_op jit(solution)/shard_map/trotter_step/pallas_call | solution.py:307
  65.9 0.0 all-reduce.2.cloned.1.call-update
  65.9 103.4 %all-reduce.2.cloned.1.call-done = f32[512,512]{1,0:T(8,128)} async-done(((f32[512,512]{1,0:T(8,128)}), f32[512,512]{1,0:T(8,128)}) %all-reduce.2.cloned.1.call-update) | async-done | bytes 1048592 | tf_op jit(solution)/shard_map/psum | solution.py:333
  169.3 0.0 copy-start.2
  169.3 4.7 %copy.12 = f32[2048,512]{1,0:T(8,128)} copy(f32[2048,512]{1,0:T(8,128)} %get-tuple-element.14) | data formatting | bytes 8388608
  174.1 0.0 copy-done.2
  174.1 1.0 copy.13
  (2 shorter events, 0.0 us)
Async XLA Ops:
  7.2 162.2 %all-reduce.2.cloned.1.call-start = ((), (), s32[]{:S(2)}) async-start(), calls=%async_computation | async-start | bytes 2097152 | tf_op jit(solution)/shard_map/psum | solution.py:333
  13.0 1.2 copy-start
  14.3 0.7 copy-start.1
  169.3 4.7 %copy-start.2 = (f32[512,512]{1,0:T(8,128)S(1)}, f32[512,512]{1,0:T(8,128)}, u32[]{:S(2)}) copy-start(f32[512,512]{1,0:T(8,128)} %all-reduce.2.cloned.1.call-done) | copy-start | bytes 3145732
Sparse Core Ops, SparseCore 0:
  66.0 103.2 all-reduce.1
where the time goes:
time: 182 us
  waiting for transfers between devices  103 us (57%)
  Pallas kernels  53.2 us (29%)
  between operations  14 us (8%)
  local copies, waits for them, and re-layouts  8.95 us (5%)
  other arithmetic  2.15 us (1%)
    psum x1, waiting for transfers between devices, per_device(): return (evolved, lax.psum(partial_value, 'rows'))  103 us
    pallas_call x1, Pallas kernels, per_device(): pl.pallas_call(functools.partial(step_kernel, devices, layers_across, lay...  50.9 us
    unnamed x8, local copies, waits for them, and re-layouts  7.64 us
  transfers between devices with their start and end apart: 1, of which 1 were waited for; matrix products, arithmetic and copies ran while one was open for 0% of the time, Pallas kernels for 0%

commit v1 on v0

--- a/solution.py
+++ b/solution.py
@@ -95,7 +95,7 @@
     coef_ref,
     edge_ref,
     evolved_ref,
-    partial_ref,
+    total_ref,
     state,
     from_last,
     from_next,
@@ -104,9 +104,18 @@
     turned,
     trial_high,
     trial_low,
+    partial,
+    from_twin,
+    half,
+    from_chips,
+    whole,
     send_sem,
     recv_sem,
     edge_sem,
+    twin_send,
+    twin_recv,
+    chip_send,
+    chip_recv,
 ):
     rows, width = coef_ref.shape[0], coef_ref.shape[1]
     chunks = state.shape[0]
@@ -115,11 +124,24 @@
     me = lax.axis_index("rows")
     after = lax.rem(me + 1, devices)
     before = lax.rem(me + devices - 1, devices)
+    side = lax.rem(me, 2)
+    twin = me + 1 - 2 * side
+    chips = devices // 2
+    chip = me // 2
+    depth = partial.shape[1] // devices
+    halves = partial.shape[1] // 2
+
+    def chip_at(distance):
+        return 2 * lax.rem(chip + distance, chips) + side
 
     barrier = pltpu.get_barrier_semaphore()
     for neighbour in (before, after):
         pl.semaphore_signal(barrier, inc=1, device_id={"rows": neighbour}, device_id_type=pl.DeviceIdType.MESH)
-    pl.semaphore_wait(barrier, 2)
+    for distance in range(1, chips):
+        pl.semaphore_signal(
+            barrier, inc=1, device_id={"rows": chip_at(distance)}, device_id_type=pl.DeviceIdType.MESH
+        )
+    pl.semaphore_wait(barrier, 1 + chips)
 
     edge_copy = pltpu.make_async_remote_copy(
         src_ref=edge_ref,
@@ -222,6 +244,75 @@
         new[rows - 1] = cosine * values[rows - 1] - sine * from_next[stage, chunk, place, :]
         return new
 
+    own_half = pl.ds(pl.multiple_of(side * halves, 8), halves)
+    other_half = pl.ds(pl.multiple_of((1 - side) * halves, 8), halves)
+    own_part = pl.ds(pl.multiple_of(side * halves + chip * depth, 8), depth)
+
+    def to_twin(chunk):
+        return pltpu.make_async_remote_copy(
+            src_ref=partial.at[chunk, other_half],
+            dst_ref=from_twin.at[chunk],
+            send_sem=twin_send.at[0, chunk],
+            recv_sem=twin_recv.at[0, chunk],
+            device_id={"rows": twin},
+            device_id_type=pl.DeviceIdType.MESH,
+        )
+
+    def to_chip(chunk, distance):
+        start = pl.multiple_of(lax.rem(chip + distance, chips) * depth, 8)
+        return pltpu.make_async_remote_copy(
+            src_ref=half.at[chunk, pl.ds(start, depth)],
+            dst_ref=from_chips.at[chunk, distance],
+            send_sem=chip_send.at[0, chunk, distance],
+            recv_sem=chip_recv.at[0, chunk, distance],
+            device_id={"rows": chip_at(distance)},
+            device_id_type=pl.DeviceIdType.MESH,
+        )
+
+    def share(chunk, distance):
+        return pltpu.make_async_remote_copy(
+            src_ref=whole.at[chunk, own_part],
+            dst_ref=whole.at[chunk, own_part],
+            send_sem=chip_send.at[1, chunk, distance],
+            recv_sem=chip_recv.at[1, chunk, distance],
+            device_id={"rows": chip_at(distance)},
+            device_id_type=pl.DeviceIdType.MESH,
+        )
+
+    def share_twin(chunk):
+        return pltpu.make_async_remote_copy(
+            src_ref=whole.at[chunk, own_half],
+            dst_ref=whole.at[chunk, own_half],
+            send_sem=twin_send.at[1, chunk],
+            recv_sem=twin_recv.at[1, chunk],
+            device_id={"rows": twin},
+            device_id_type=pl.DeviceIdType.MESH,
+        )
+
+    def sum_twin(chunk):
+        to_twin(chunk).wait()
+        half[chunk] = partial[chunk, own_half, :] + from_twin[chunk]
+        for distance in range(1, chips):
+            to_chip(chunk, distance).start()
+
+    def sum_chips(chunk):
+        total = half[chunk, pl.ds(pl.multiple_of(chip * depth, 8), depth), :]
+        for distance in range(1, chips):
+            to_chip(chunk, distance).wait()
+            total = total + from_chips[chunk, distance]
+        whole[chunk, own_part, :] = total
+        for distance in range(1, chips):
+            share(chunk, distance).start()
+
+    def gather_chips(chunk):
+        for distance in range(1, chips):
+            share(chunk, distance).wait()
+        share_twin(chunk).start()
+
+    def gather_twin(chunk):
+        share_twin(chunk).wait()
+        total_ref[:, columns_of(chunk)] = whole[chunk]
+
     for stage in range(stages):
         final = stage == stages - 1
 
@@ -256,17 +347,28 @@
                 for copy in exchange(stage + 1, chunk):
                     copy.start()
                 return carry
-            total = jnp.zeros((partial_ref.shape[0], LANES), jnp.float32)
+            total = jnp.zeros((partial.shape[1], LANES), jnp.float32)
             for row in range(rows):
                 place = pl.ds(row * width, width)
                 high, low = split(evolved_ref[place, columns_of(chunk)])
                 total += jnp.dot(trial_high[:, place], high, preferred_element_type=jnp.float32)
                 total += jnp.dot(trial_high[:, place], low, preferred_element_type=jnp.float32)
                 total += jnp.dot(trial_low[:, place], high, preferred_element_type=jnp.float32)
-            partial_ref[:, columns_of(chunk)] = total
+            partial[chunk] = total
+            to_twin(chunk).start()
             return carry
 
-        lax.fori_loop(0, chunks, advance, 0)
+        if not final:
+            lax.fori_loop(0, chunks, advance, 0)
+            continue
+
+        def flow(turn, carry):
+            pl.when(turn < chunks)(lambda: advance(turn, None))
+            for late, work in enumerate((sum_twin, sum_chips, gather_chips, gather_twin), 1):
+                pl.when((turn >= late) & (turn < chunks + late))(functools.partial(work, turn - late))
+            return carry
+
+        lax.fori_loop(0, chunks + 4, flow, 0)
 
 
 def per_device(
@@ -304,7 +406,7 @@
     )(code, jnp.cos(angles)[None, :], jnp.sin(angles)[None, :])
 
     in_vmem = pl.BlockSpec(memory_space=pltpu.VMEM)
-    evolved, partial_value = pl.pallas_call(
+    return pl.pallas_call(
         functools.partial(step_kernel, devices, layers_across, layers_up),
         out_shape=(
             jax.ShapeDtypeStruct((modes, columns), jnp.float32),
@@ -321,16 +423,24 @@
             pltpu.VMEM((rows, width, LANES), jnp.float32),
             pltpu.VMEM((trials, modes), jnp.bfloat16),
             pltpu.VMEM((trials, modes), jnp.bfloat16),
+            pltpu.VMEM((chunks, trials, LANES), jnp.float32),
+            pltpu.VMEM((chunks, trials // 2, LANES), jnp.float32),
+            pltpu.VMEM((chunks, trials // 2, LANES), jnp.float32),
+            pltpu.VMEM((chunks, devices // 2, trials // devices, LANES), jnp.float32),
+            pltpu.VMEM((chunks, trials, LANES), jnp.float32),
             pltpu.SemaphoreType.DMA((stages, 2, chunks)),
             pltpu.SemaphoreType.DMA((stages, 2, chunks)),
             pltpu.SemaphoreType.DMA((2,)),
+            pltpu.SemaphoreType.DMA((2, chunks)),
+            pltpu.SemaphoreType.DMA((2, chunks)),
+            pltpu.SemaphoreType.DMA((2, chunks, devices // 2)),
+            pltpu.SemaphoreType.DMA((2, chunks, devices // 2)),
         ],
         compiler_params=pltpu.CompilerParams(
             collective_id=0, has_side_effects=True, vmem_limit_bytes=50 * 1024 * 1024
         ),
         name="trotter_step",
     )(orbitals, trial_orbitals, coef, edge)
-    return evolved, lax.psum(partial_value, "rows")
 
 
 def solution(mesh):

time: 182 us -> 99.1 us (0.54)
  waiting for transfers between devices: 103 us -> 0 us
  Pallas kernels: 53.2 us -> 87 us
  between operations: 14 us -> 0.65 us
    psum x1 -> x0, waiting for transfers between devices: 103 us -> none  [per_device(): return (evolved, lax.psum(partial_value, 'rows'))]
    pallas_call x1, Pallas kernels: 50.9 us -> 84.6 us  [per_device(): pl.pallas_call(functools.partial(step_kernel, devices, layers_across, lay...]
    unnamed x8 -> x6, local copies, waits for them, and re-layouts: 7.64 us -> 7.55 us
  transfers between devices with their start and end apart: 1 -> 0, of which waited for: 1 -> 0; matrix products, arithmetic and copies ran while one was open for 0% -> 0% of each run, Pallas kernels for 0% -> 0%
where the time goes in v1:
time: 99.1 us; the launch traced here: 98.6 us
  Pallas kernels  87 us (88%)
  local copies, waits for them, and re-layouts  8.87 us (9%)
  other arithmetic  2.15 us (2%)
    pallas_call x1, Pallas kernels, per_device(): pl.pallas_call(functools.partial(step_kernel, devices, layers_across, lay...  84.6 us
    unnamed x6, local copies, waits for them, and re-layouts  7.55 us
    pallas_call x1, Pallas kernels, per_device(): pl.pallas_call(functools.partial(coefficient_kernel, layers_across, layer...  2.34 us

profile of v1, /device:TPU:0, one launch (start us, length us, event | category | flops | bytes accessed | tf_op | source)
XLA Modules:
  0.0 98.6 jit_solution(3139877243108641516)
XLA Ops:
  0.6 1.3 %sine_bitcast_fusion = (f32[1,128]{1,0:T(1,128)}, f32[1,128]{1,0:T(1,128)}) fusion(f32[128]{0:T(128)} %param.9), kind=kLoop, calls=%fused_computation.3 | loop fusion | bytes 1536 | tf_op jit(solution)/shard_map/broadcast_in_dim | solution.py:406
  1.9 0.7 compare_select_fusion.1
  2.7 0.8 compare_select_fusion
  3.5 0.6 pad_add_fusion.code_ref
  4.1 2.3 %coefficients.1 = (f32[4,512,16]{2,1,0:T(8,128)}, f32[8,512]{1,0:T(8,128)}) custom-call(s32[24,512]{1,0:T(8,128)} %pad_add_fusion.code_ref, f32[1,128]{1,0:T(1,128)} %get-tuple-element.7.cos_ref, f32[1,128]{1,0:T(1,128)} %get-tuple-element.6.sin_ref), custom_call_target="tpu_custom_call" | custom-call | tf_op jit(solution)/shard_map/coefficients/pallas_call | solution.py:399
  6.5 0.0 copy-start
  6.5 1.2 %copy-done = f32[4,512,16]{2,1,0:T(8,128)S(1)} copy-done((f32[4,512,16]{2,1,0:T(8,128)S(1)}, f32[4,512,16]{2,1,0:T(8,128)}, u32[]{:S(2)}) %copy-start) | copy-done | bytes 131096
  7.7 0.0 copy-start.1
  7.7 0.7 copy-done.1
  8.4 84.6 %trotter_step.1 = (f32[2048,512]{1,0:T(8,128)}, f32[512,512]{1,0:T(8,128)S(1)}) custom-call(f32[2048,512]{1,0:T(8,128)} %orbital_ref.1, f32[2048,512]{1,0:T(8,128)} %trial_ref.1, f32[4,512,16]{2,1,0:T(8,128)S(1)} %copy-done, f32[8,512]{1,0:T(8,128)S(1)} %copy-done.1), custom_call_target="tpu_custom_call" | custom-call | tf_op jit(solution)/shard_map/trotter_step/pallas_call | solution.py:409
  93.0 4.6 %copy.11 = f32[2048,512]{1,0:T(8,128)} copy(f32[2048,512]{1,0:T(8,128)} %get-tuple-element.10) | data formatting | bytes 8388608
  97.7 1.0 copy.12
  (2 shorter events, 0.0 us)
Async XLA Ops:
  6.5 1.2 %copy-start = (f32[4,512,16]{2,1,0:T(8,128)S(1)}, f32[4,512,16]{2,1,0:T(8,128)}, u32[]{:S(2)}) copy-start(f32[4,512,16]{2,1,0:T(8,128)} %get-tuple-element.4.coef_ref) | copy-start | bytes 393220
  7.7 0.7 copy-start.1

commit v2 on v1

--- a/solution.py
+++ b/solution.py
@@ -9,14 +9,26 @@
 
 LANES = 128
 BLOCK = 64
-
-
-def coefficient_kernel(layers_across, layers_up, rows, code_ref, cos_ref, sin_ref, coef_ref, edge_ref):
-    count, width = code_ref.shape
+IN_FLIGHT = 2
+
+
+def coefficient_kernel(layers_across, layers_up, rows, across_index, across_mask, up_index, up_mask, cos_ref, sin_ref, coef_ref, edge_ref):
+    code_all = jnp.concatenate(
+        [
+            jnp.where(mask[layer] == 1, index[layer], -1)
+            for index, mask, layers in (
+                (across_index, across_mask, layers_across),
+                (up_index, up_mask, layers_up),
+            )
+            for layer in range(layers)
+        ],
+        axis=0,
+    )
+    count, width = code_all.shape
     blocks = width // LANES
     cosines, sines = [], []
     for block in range(blocks):
-        code = code_ref[:, block * LANES : (block + 1) * LANES]
+        code = code_all[:, block * LANES : (block + 1) * LANES]
         place = jnp.maximum(code, 0)
         table_cos = jnp.broadcast_to(cos_ref[...], code.shape)
         table_sin = jnp.broadcast_to(sin_ref[...], code.shape)
@@ -90,8 +102,8 @@
     devices,
     layers_across,
     layers_up,
-    orbital_ref,
-    trial_ref,
+    orbital_source,
+    trial_source,
     coef_ref,
     edge_ref,
     evolved_ref,
@@ -102,12 +114,16 @@
     edge_in,
     edge_coef,
     turned,
+    wide_across,
+    wide_up,
     trial_high,
     trial_low,
     partial,
     from_twin,
     half,
     from_chips,
+    own,
+    from_near,
     whole,
     send_sem,
     recv_sem,
@@ -116,6 +132,10 @@
     twin_recv,
     chip_send,
     chip_recv,
+    near_sem,
+    orbital_ref,
+    trial_ref,
+    load_sem,
 ):
     rows, width = coef_ref.shape[0], coef_ref.shape[1]
     chunks = state.shape[0]
@@ -126,22 +146,37 @@
     before = lax.rem(me + devices - 1, devices)
     side = lax.rem(me, 2)
     twin = me + 1 - 2 * side
-    chips = devices // 2
-    chip = me // 2
-    depth = partial.shape[1] // devices
+    far_count = devices // 4
+    far = me // 4
+    near = lax.rem(me // 2, 2)
+    opposite = me + 2 - 4 * near
+    depth = partial.shape[1] // 2 // far_count
     halves = partial.shape[1] // 2
 
     def chip_at(distance):
-        return 2 * lax.rem(chip + distance, chips) + side
+        return 4 * lax.rem(far + distance, far_count) + 2 * near + side
+
+    def columns_of(chunk):
+        return pl.ds(pl.multiple_of(chunk * LANES, LANES), LANES)
+
+    def load(chunk):
+        return pltpu.make_async_copy(
+            orbital_source.at[:, columns_of(chunk)], orbital_ref.at[chunk], load_sem.at[chunk]
+        )
+
+    load_trial = pltpu.make_async_copy(trial_source, trial_ref, load_sem.at[chunks])
+    for chunk in range(chunks):
+        load(chunk).start()
+    load_trial.start()
 
     barrier = pltpu.get_barrier_semaphore()
-    for neighbour in (before, after):
+    for neighbour in (before, after, opposite):
         pl.semaphore_signal(barrier, inc=1, device_id={"rows": neighbour}, device_id_type=pl.DeviceIdType.MESH)
-    for distance in range(1, chips):
+    for distance in range(1, far_count):
         pl.semaphore_signal(
             barrier, inc=1, device_id={"rows": chip_at(distance)}, device_id_type=pl.DeviceIdType.MESH
         )
-    pl.semaphore_wait(barrier, 1 + chips)
+    pl.semaphore_wait(barrier, 2 + far_count)
 
     edge_copy = pltpu.make_async_remote_copy(
         src_ref=edge_ref,
@@ -172,47 +207,92 @@
         )
         return down, up
 
-    def columns_of(chunk):
-        return pl.ds(pl.multiple_of(chunk * LANES, LANES), LANES)
+    def begin(stage, chunk):
+        for copy in exchange(stage, chunk):
+            copy.start()
+
+    def widen(line, shape=(BLOCK, LANES)):
+        return jnp.broadcast_to(line, shape)
+
+    def widen_vertical(layer, row, place):
+        lane = 2 * (layers_across + layer)
+        for part in range(2):
+            line = coef_ref[row, place, :][:, lane + part : lane + part + 1]
+            wide_up[layer, (row + 1) // 2, part, place, :] = widen(line)
 
     def vertical(row, layer, place):
-        lane = 2 * (layers_across + layer)
-        pair = coef_ref[row, place, :]
-        return pair[:, lane : lane + 1], pair[:, lane + 1 : lane + 2]
+        slot = (row + 1) // 2
+        return wide_up[layer, slot, 0, place, :], wide_up[layer, slot, 1, place, :]
+
+    def block_at(step):
+        return pl.ds(pl.multiple_of(step * BLOCK, BLOCK), BLOCK)
+
+    def prepare(step, carry):
+        place = block_at(step)
+        for row in range(rows):
+            lines = coef_ref[row, place, :]
+            for lane in range(2 * layers_across):
+                wide_across[row, lane, place, :] = widen(lines[:, lane : lane + 1])
+            if row % 2 == 0:
+                widen_vertical(0, row, place)
+        return carry
+
+    lax.fori_loop(0, steps, prepare, 0)
+    turned[:, :, :8, :] = jnp.zeros((turned.shape[0], rows, 8, LANES), jnp.float32)
+    turned[:, :, width + 8 :, :] = jnp.zeros((turned.shape[0], rows, 8, LANES), jnp.float32)
+
+    def across(layer, row, start, chunk):
+        if layer == 0:
+            value = orbital_ref[chunk, pl.ds(pl.multiple_of(row * width + start, BLOCK), BLOCK), :]
+        elif layer % 2 == 0:
+            value = turned[layer - 1, row, pl.ds(pl.multiple_of(8 + start, 8), BLOCK), :]
+        else:
+            value = turned[layer - 1, row, pl.ds(pl.multiple_of(start, 8), BLOCK + 16), :]
+        if layer % 2 == 0:
+            view = value.reshape(BLOCK // 8, 8, LANES)
+            place = lax.broadcasted_iota(jnp.int32, view.shape, 1)
+            partner = jnp.where(place % 2 == 0, pltpu.roll(view, 7, 1), pltpu.roll(view, 1, 1))
+            partner = partner.reshape(BLOCK, LANES)
+        else:
+            place = lax.broadcasted_iota(jnp.int32, value.shape, 0)
+            partner = jnp.where(place % 2 == 1, pltpu.roll(value, BLOCK + 15, 0), pltpu.roll(value, 1, 0))
+            partner = partner[8 : 8 + BLOCK]
+            value = value[8 : 8 + BLOCK]
+        at = pl.ds(pl.multiple_of(start, BLOCK), BLOCK)
+        return wide_across[row, 2 * layer, at, :] * value + wide_across[row, 2 * layer + 1, at, :] * partner
 
     def open_chunk(chunk, carry):
-        columns = columns_of(chunk)
-        position = lax.broadcasted_iota(jnp.int32, (width, LANES), 0)
-        for row in range(rows):
-            value = orbital_ref[pl.ds(row * width, width), columns]
-            for layer in range(layers_across):
-                diagonal = coef_ref[row, :, 2 * layer : 2 * layer + 1]
-                beside = coef_ref[row, :, 2 * layer + 1 : 2 * layer + 2]
-                partner = jnp.where(
-                    position % 2 == layer % 2, pltpu.roll(value, width - 1, 0), pltpu.roll(value, 1, 0)
-                )
-                value = diagonal * value + beside * partner
-            turned[row] = value
+        load(chunk).wait()
+        for layer in range(layers_across - 1):
+
+            def inner(step, carry):
+                start = step * BLOCK
+                for row in range(rows):
+                    at = pl.ds(pl.multiple_of(8 + start, 8), BLOCK)
+                    turned[layer, row, at, :] = across(layer, row, start, chunk)
+                return carry
+
+            lax.fori_loop(0, steps, inner, 0)
 
         def pairs(step, carry):
-            start = pl.multiple_of(step * BLOCK, BLOCK)
-            mirrored = pl.multiple_of(width - BLOCK - step * BLOCK, BLOCK)
-            place = pl.ds(start, BLOCK)
+            start = step * BLOCK
+            mirrored = width - BLOCK - start
+            place = block_at(step)
             for row in range(0, rows, 2):
-                lower = turned[row, place, :]
-                upper = flip(turned[row + 1, pl.ds(mirrored, BLOCK), :])
+                lower = across(layers_across - 1, row, start, chunk)
+                upper = flip(across(layers_across - 1, row + 1, mirrored, chunk))
                 cosine, sine = vertical(row, 0, place)
                 state[chunk, row, place, :] = cosine * lower - sine * upper
                 state[chunk, row + 1, place, :] = sine * lower + cosine * upper
             return carry
 
         lax.fori_loop(0, steps, pairs, 0)
-        for copy in exchange(0, chunk):
-            copy.start()
+        pl.when(chunk < IN_FLIGHT)(functools.partial(begin, 0, chunk))
         return carry
 
     lax.fori_loop(0, chunks, open_chunk, 0)
 
+    load_trial.wait()
     for row in range(rows):
         place = pl.ds(row * width, width)
 
@@ -228,12 +308,24 @@
     edge_copy.wait()
     edge_coef[...] = jnp.transpose(edge_in[...])
 
+    def prepare_later(step, carry):
+        place = block_at(step)
+        edge = edge_coef[place, :]
+        for layer in range(1, layers_up):
+            for row in range(layer % 2, rows, 2):
+                widen_vertical(layer, row, place)
+            if layer % 2:
+                for part in range(2):
+                    lane = layer - 1 + part
+                    wide_up[layer, 0, part, place, :] = widen(edge[:, lane : lane + 1])
+        return carry
+
+    lax.fori_loop(0, steps, prepare_later, 0)
+
     def crossing(stage, chunk, place):
         layer = 2 * stage + 1
         values = [state[chunk, row, place, :] for row in range(rows)]
-        edge = edge_coef[place, :]
-        edge_cos = edge[:, 2 * stage : 2 * stage + 1]
-        edge_sin = edge[:, 2 * stage + 1 : 2 * stage + 2]
+        edge_cos, edge_sin = vertical(0, layer, place)
         new = list(values)
         new[0] = edge_sin * from_last[stage, chunk, place, :] + edge_cos * values[0]
         for row in range(1, rows - 1, 2):
@@ -246,7 +338,7 @@
 
     own_half = pl.ds(pl.multiple_of(side * halves, 8), halves)
     other_half = pl.ds(pl.multiple_of((1 - side) * halves, 8), halves)
-    own_part = pl.ds(pl.multiple_of(side * halves + chip * depth, 8), depth)
+    own_part = pl.ds(pl.multiple_of(side * halves + far * depth, 8), depth)
 
     def to_twin(chunk):
         return pltpu.make_async_remote_copy(
@@ -259,13 +351,23 @@
         )
 
     def to_chip(chunk, distance):
-        start = pl.multiple_of(lax.rem(chip + distance, chips) * depth, 8)
+        start = pl.multiple_of(lax.rem(far + distance, far_count) * depth, 8)
         return pltpu.make_async_remote_copy(
             src_ref=half.at[chunk, pl.ds(start, depth)],
             dst_ref=from_chips.at[chunk, distance],
             send_sem=chip_send.at[0, chunk, distance],
             recv_sem=chip_recv.at[0, chunk, distance],
             device_id={"rows": chip_at(distance)},
+            device_id_type=pl.DeviceIdType.MESH,
+        )
+
+    def cross(chunk):
+        return pltpu.make_async_remote_copy(
+            src_ref=own.at[chunk],
+            dst_ref=from_near.at[chunk],
+            send_sem=near_sem.at[0, chunk],
+            recv_sem=near_sem.at[1, chunk],
+            device_id={"rows": opposite},
             device_id_type=pl.DeviceIdType.MESH,
         )
 
@@ -292,20 +394,25 @@
     def sum_twin(chunk):
         to_twin(chunk).wait()
         half[chunk] = partial[chunk, own_half, :] + from_twin[chunk]
-        for distance in range(1, chips):
+        for distance in range(1, far_count):
             to_chip(chunk, distance).start()
 
     def sum_chips(chunk):
-        total = half[chunk, pl.ds(pl.multiple_of(chip * depth, 8), depth), :]
-        for distance in range(1, chips):
+        total = half[chunk, pl.ds(pl.multiple_of(far * depth, 8), depth), :]
+        for distance in range(1, far_count):
             to_chip(chunk, distance).wait()
             total = total + from_chips[chunk, distance]
-        whole[chunk, own_part, :] = total
-        for distance in range(1, chips):
+        own[chunk] = total
+        cross(chunk).start()
+
+    def sum_near(chunk):
+        cross(chunk).wait()
+        whole[chunk, own_part, :] = own[chunk] + from_near[chunk]
+        for distance in range(1, far_count):
             share(chunk, distance).start()
 
     def gather_chips(chunk):
-        for distance in range(1, chips):
+        for distance in range(1, far_count):
             share(chunk, distance).wait()
         share_twin(chunk).start()
 
@@ -319,6 +426,10 @@
         def advance(chunk, carry):
             for copy in exchange(stage, chunk):
                 copy.wait()
+            later = chunk + IN_FLIGHT
+            pl.when(later < chunks)(functools.partial(begin, stage, later))
+            if not final:
+                pl.when(later >= chunks)(functools.partial(begin, stage + 1, later - chunks))
 
             def middle(step, carry):
                 place = pl.ds(pl.multiple_of(step * BLOCK, BLOCK), BLOCK)
@@ -344,15 +455,14 @@
 
             lax.fori_loop(0, steps, close if final else middle, 0)
             if not final:
-                for copy in exchange(stage + 1, chunk):
-                    copy.start()
                 return carry
             total = jnp.zeros((partial.shape[1], LANES), jnp.float32)
             for row in range(rows):
                 place = pl.ds(row * width, width)
                 high, low = split(evolved_ref[place, columns_of(chunk)])
-                total += jnp.dot(trial_high[:, place], high, preferred_element_type=jnp.float32)
-                total += jnp.dot(trial_high[:, place], low, preferred_element_type=jnp.float32)
+                both = jnp.concatenate([high, low], axis=1)
+                both = jnp.dot(trial_high[:, place], both, preferred_element_type=jnp.float32)
+                total += both[:, :LANES] + both[:, LANES:]
                 total += jnp.dot(trial_low[:, place], high, preferred_element_type=jnp.float32)
             partial[chunk] = total
             to_twin(chunk).start()
@@ -364,11 +474,11 @@
 
         def flow(turn, carry):
             pl.when(turn < chunks)(lambda: advance(turn, None))
-            for late, work in enumerate((sum_twin, sum_chips, gather_chips, gather_twin), 1):
+            for late, work in enumerate((sum_twin, sum_chips, sum_near, gather_chips, gather_twin), 1):
                 pl.when((turn >= late) & (turn < chunks + late))(functools.partial(work, turn - late))
             return carry
 
-        lax.fori_loop(0, chunks + 4, flow, 0)
+        lax.fori_loop(0, chunks + 5, flow, 0)
 
 
 def per_device(
@@ -386,14 +496,8 @@
     modes, columns = orbitals.shape
     trials = trial_orbitals.shape[1]
     chunks = columns // LANES
+    far_count = devices // 4
     stages = layers_up // 2
-    code = jnp.concatenate(
-        [
-            jnp.where(horizontal_mask == 1, horizontal_index, -1).reshape(layers_across * rows, width),
-            jnp.where(vertical_mask == 1, vertical_index, -1).reshape(layers_up * rows, width),
-        ],
-        axis=0,
-    )
     lanes = -(-2 * (layers_across + layers_up) // 8) * 8
     edges = -(-2 * stages // 8) * 8
     coef, edge = pl.pallas_call(
@@ -403,16 +507,24 @@
             jax.ShapeDtypeStruct((edges, width), jnp.float32),
         ),
         name="coefficients",
-    )(code, jnp.cos(angles)[None, :], jnp.sin(angles)[None, :])
+    )(
+        horizontal_index,
+        horizontal_mask,
+        vertical_index,
+        vertical_mask,
+        jnp.cos(angles)[None, :],
+        jnp.sin(angles)[None, :],
+    )
 
     in_vmem = pl.BlockSpec(memory_space=pltpu.VMEM)
+    in_hbm = pl.BlockSpec(memory_space=pl.ANY)
     return pl.pallas_call(
         functools.partial(step_kernel, devices, layers_across, layers_up),
         out_shape=(
             jax.ShapeDtypeStruct((modes, columns), jnp.float32),
             jax.ShapeDtypeStruct((trials, columns), jnp.float32),
         ),
-        in_specs=[in_vmem] * 4,
+        in_specs=[in_hbm, in_hbm, in_vmem, in_vmem],
         out_specs=(in_vmem, in_vmem),
         scratch_shapes=[
             pltpu.VMEM((chunks, rows, width, LANES), jnp.float32),
@@ -420,24 +532,32 @@
             pltpu.VMEM((stages, chunks, width, LANES), jnp.float32),
             pltpu.VMEM((edges, width), jnp.float32),
             pltpu.VMEM((width, edges), jnp.float32),
-            pltpu.VMEM((rows, width, LANES), jnp.float32),
+            pltpu.VMEM((max(layers_across - 1, 1), rows, width + 16, LANES), jnp.float32),
+            pltpu.VMEM((rows, 2 * layers_across, width, LANES), jnp.float32),
+            pltpu.VMEM((layers_up, rows // 2 + 1, 2, width, LANES), jnp.float32),
             pltpu.VMEM((trials, modes), jnp.bfloat16),
             pltpu.VMEM((trials, modes), jnp.bfloat16),
             pltpu.VMEM((chunks, trials, LANES), jnp.float32),
             pltpu.VMEM((chunks, trials // 2, LANES), jnp.float32),
             pltpu.VMEM((chunks, trials // 2, LANES), jnp.float32),
-            pltpu.VMEM((chunks, devices // 2, trials // devices, LANES), jnp.float32),
+            pltpu.VMEM((chunks, far_count, trials // 2 // far_count, LANES), jnp.float32),
+            pltpu.VMEM((chunks, trials // 2 // far_count, LANES), jnp.float32),
+            pltpu.VMEM((chunks, trials // 2 // far_count, LANES), jnp.float32),
             pltpu.VMEM((chunks, trials, LANES), jnp.float32),
             pltpu.SemaphoreType.DMA((stages, 2, chunks)),
             pltpu.SemaphoreType.DMA((stages, 2, chunks)),
             pltpu.SemaphoreType.DMA((2,)),
             pltpu.SemaphoreType.DMA((2, chunks)),
             pltpu.SemaphoreType.DMA((2, chunks)),
-            pltpu.SemaphoreType.DMA((2, chunks, devices // 2)),
-            pltpu.SemaphoreType.DMA((2, chunks, devices // 2)),
+            pltpu.SemaphoreType.DMA((2, chunks, far_count)),
+            pltpu.SemaphoreType.DMA((2, chunks, far_count)),
+            pltpu.SemaphoreType.DMA((2, chunks)),
+            pltpu.VMEM((chunks, modes, LANES), jnp.float32),
+            pltpu.VMEM((modes, trials), jnp.float32),
+            pltpu.SemaphoreType.DMA((chunks + 1,)),
         ],
         compiler_params=pltpu.CompilerParams(
-            collective_id=0, has_side_effects=True, vmem_limit_bytes=50 * 1024 * 1024
+            collective_id=0, has_side_effects=True, vmem_limit_bytes=56 * 1024 * 1024
         ),
         name="trotter_step",
     )(orbitals, trial_orbitals, coef, edge)

time: 99.1 us -> 91.6 us (0.924)
  Pallas kernels: 87 us -> 83.8 us
  other arithmetic: 2.15 us -> 0 us
  local copies, waits for them, and re-layouts: 8.87 us -> 6.94 us
    pallas_call x1, Pallas kernels: 84.6 us -> 81.4 us  [per_device(): pl.pallas_call(functools.partial(step_kernel, devices, layers_across, lay...]
    unnamed x6 -> x4, local copies, waits for them, and re-layouts: 7.55 us -> 5.7 us
    select_n x2 -> x0, other arithmetic: 1.53 us -> none  [the longest x1 0.79 us: per_device(): jnp.where(vertical_mask == 1, vertical_index, -1)]
where the time goes in v2:
time: 91.6 us; the launch traced here: 91.4 us
  Pallas kernels  83.8 us (91%)
  local copies, waits for them, and re-layouts  6.94 us (8%)
    pallas_call x1, Pallas kernels, per_device(): pl.pallas_call(functools.partial(step_kernel, devices, layers_across, lay...  81.4 us
    unnamed x4, local copies, waits for them, and re-layouts  5.7 us
    pallas_call x1, Pallas kernels, per_device(): pl.pallas_call(functools.partial(coefficient_kernel, layers_across, layer...  2.35 us

profile of v2, /device:TPU:0, one launch (start us, length us, event | category | flops | bytes accessed | tf_op | source)
XLA Modules:
  0.0 91.4 jit_solution(6896029279029070377)
XLA Ops:
  0.6 1.2 %sine_bitcast_fusion = (f32[1,128]{1,0:T(1,128)}, f32[1,128]{1,0:T(1,128)}) fusion(f32[128]{0:T(128)} %param.9), kind=kLoop, calls=%fused_computation | loop fusion | bytes 1536 | tf_op jit(solution)/shard_map/broadcast_in_dim | solution.py:516
  1.9 2.4 %coefficients.1 = (f32[4,512,16]{2,1,0:T(8,128)}, f32[8,512]{1,0:T(8,128)}) custom-call(s32[2,4,512]{2,1,0:T(4,128)} %across_index.1, s32[2,4,512]{2,1,0:T(4,128)} %across_mask.1, s32[4,4,512]{2,1,0:T(4,128)} %up_index.1, s32[4,4,512]{2,1,0:T(4,128)} %up_mask.1, f32[1,128]{1,0:T(1,128)} %get-tuple-element.7.cos_ref, f32[1,128]{1,0:T(1,128)} %get-tuple-element.6.sin_ref), custom_call_target="tpu_custom_call" | custom-call | tf_op jit(solution)/shard_map/coefficients/pallas_call | solution.py:503
  4.2 81.4 %trotter_step.1 = (f32[2048,512]{1,0:T(8,128)}, f32[512,512]{1,0:T(8,128)}) custom-call(f32[2048,512]{1,0:T(8,128)} %orbital_source.1, f32[2048,512]{1,0:T(8,128)} %trial_source.1, f32[4,512,16]{2,1,0:T(8,128)} %get-tuple-element.4.coef_ref, f32[8,512]{1,0:T(8,128)} %get-tuple-element.5.edge_ref), custom_call_target="tpu_custom_call" | custom-call | tf_op jit(solution)/shard_map/trotter_step/pallas_call | solution.py:521
  85.7 0.0 copy-start
  85.7 4.7 %copy.11 = f32[2048,512]{1,0:T(8,128)} copy(f32[2048,512]{1,0:T(8,128)} %get-tuple-element.10) | data formatting | bytes 8388608
  90.4 0.0 copy-done
  90.4 1.0 %copy.12 = f32[512,512]{1,0:T(8,128)} copy(f32[512,512]{1,0:T(8,128)S(1)} %copy-done) | data formatting | bytes 2097152
Async XLA Ops:
  85.7 4.7 %copy-start = (f32[512,512]{1,0:T(8,128)S(1)}, f32[512,512]{1,0:T(8,128)}, u32[]{:S(2)}) copy-start(f32[512,512]{1,0:T(8,128)} %get-tuple-element.11) | copy-start | bytes 3145732

commit v3 on v2

--- a/solution.py
+++ b/solution.py
@@ -8,8 +8,8 @@
 from jax.sharding import PartitionSpec as P
 
 LANES = 128
-BLOCK = 64
-IN_FLIGHT = 2
+BLOCK = 128
+IN_FLIGHT = 3
 
 
 def coefficient_kernel(layers_across, layers_up, rows, across_index, across_mask, up_index, up_mask, cos_ref, sin_ref, coef_ref, edge_ref):
@@ -106,7 +106,7 @@
     trial_source,
     coef_ref,
     edge_ref,
-    evolved_ref,
+    evolved_target,
     total_ref,
     state,
     from_last,
@@ -136,6 +136,8 @@
     orbital_ref,
     trial_ref,
     load_sem,
+    evolved_ref,
+    store_sem,
 ):
     rows, width = coef_ref.shape[0], coef_ref.shape[1]
     chunks = state.shape[0]
@@ -162,6 +164,11 @@
     def load(chunk):
         return pltpu.make_async_copy(
             orbital_source.at[:, columns_of(chunk)], orbital_ref.at[chunk], load_sem.at[chunk]
+        )
+
+    def store(chunk):
+        return pltpu.make_async_copy(
+            evolved_ref.at[chunk], evolved_target.at[:, columns_of(chunk)], store_sem.at[chunk]
         )
 
     load_trial = pltpu.make_async_copy(trial_source, trial_ref, load_sem.at[chunks])
@@ -447,19 +454,20 @@
                 for row in range(rows):
                     if row % 2:
                         at = pl.ds(pl.multiple_of((row + 1) * width - BLOCK - start, BLOCK), BLOCK)
-                        evolved_ref[at, columns_of(chunk)] = flip(new[row])
+                        evolved_ref[chunk, at, :] = flip(new[row])
                     else:
                         at = pl.ds(pl.multiple_of(row * width + start, BLOCK), BLOCK)
-                        evolved_ref[at, columns_of(chunk)] = new[row]
+                        evolved_ref[chunk, at, :] = new[row]
                 return carry
 
             lax.fori_loop(0, steps, close if final else middle, 0)
             if not final:
                 return carry
+            store(chunk).start()
             total = jnp.zeros((partial.shape[1], LANES), jnp.float32)
             for row in range(rows):
                 place = pl.ds(row * width, width)
-                high, low = split(evolved_ref[place, columns_of(chunk)])
+                high, low = split(evolved_ref[chunk, place, :])
                 both = jnp.concatenate([high, low], axis=1)
                 both = jnp.dot(trial_high[:, place], both, preferred_element_type=jnp.float32)
                 total += both[:, :LANES] + both[:, LANES:]
@@ -479,6 +487,8 @@
             return carry
 
         lax.fori_loop(0, chunks + 5, flow, 0)
+        for chunk in range(chunks):
+            store(chunk).wait()
 
 
 def per_device(
@@ -525,7 +535,7 @@
             jax.ShapeDtypeStruct((trials, columns), jnp.float32),
         ),
         in_specs=[in_hbm, in_hbm, in_vmem, in_vmem],
-        out_specs=(in_vmem, in_vmem),
+        out_specs=(in_hbm, in_vmem),
         scratch_shapes=[
             pltpu.VMEM((chunks, rows, width, LANES), jnp.float32),
             pltpu.VMEM((stages, chunks, width, LANES), jnp.float32),
@@ -555,6 +565,8 @@
             pltpu.VMEM((chunks, modes, LANES), jnp.float32),
             pltpu.VMEM((modes, trials), jnp.float32),
             pltpu.SemaphoreType.DMA((chunks + 1,)),
+            pltpu.VMEM((chunks, modes, LANES), jnp.float32),
+            pltpu.SemaphoreType.DMA((chunks,)),
         ],
         compiler_params=pltpu.CompilerParams(
             collective_id=0, has_side_effects=True, vmem_limit_bytes=56 * 1024 * 1024

time: 91.6 us -> 89.7 us (0.979)
  Pallas kernels: 83.8 us -> 81.8 us
    pallas_call x1, Pallas kernels: 81.4 us -> 79.5 us  [per_device(): pl.pallas_call(functools.partial(step_kernel, devices, layers_across, lay...]
where the time goes in v3:
time: 89.7 us; the launch traced here: 89.4 us
  Pallas kernels  81.8 us (91%)
  local copies, waits for them, and re-layouts  6.94 us (8%)
    pallas_call x1, Pallas kernels, per_device(): pl.pallas_call(functools.partial(step_kernel, devices, layers_across, lay...  79.5 us
    unnamed x4, local copies, waits for them, and re-layouts  5.7 us
    pallas_call x1, Pallas kernels, per_device(): pl.pallas_call(functools.partial(coefficient_kernel, layers_across, layer...  2.35 us

profile of v3, /device:TPU:0, one launch (start us, length us, event | category | flops | bytes accessed | tf_op | source)
XLA Modules:
  0.0 89.4 jit_solution(15924785777524857584)
XLA Ops:
  0.6 1.2 %sine_bitcast_fusion = (f32[1,128]{1,0:T(1,128)}, f32[1,128]{1,0:T(1,128)}) fusion(f32[128]{0:T(128)} %param.9), kind=kLoop, calls=%fused_computation | loop fusion | bytes 1536 | tf_op jit(solution)/shard_map/broadcast_in_dim | solution.py:526
  1.9 2.4 %coefficients.1 = (f32[4,512,16]{2,1,0:T(8,128)}, f32[8,512]{1,0:T(8,128)}) custom-call(s32[2,4,512]{2,1,0:T(4,128)} %across_index.1, s32[2,4,512]{2,1,0:T(4,128)} %across_mask.1, s32[4,4,512]{2,1,0:T(4,128)} %up_index.1, s32[4,4,512]{2,1,0:T(4,128)} %up_mask.1, f32[1,128]{1,0:T(1,128)} %get-tuple-element.7.cos_ref, f32[1,128]{1,0:T(1,128)} %get-tuple-element.6.sin_ref), custom_call_target="tpu_custom_call" | custom-call | tf_op jit(solution)/shard_map/coefficients/pallas_call | solution.py:513
  4.2 79.5 %trotter_step.1 = (f32[2048,512]{1,0:T(8,128)}, f32[512,512]{1,0:T(8,128)}) custom-call(f32[2048,512]{1,0:T(8,128)} %orbital_source.1, f32[2048,512]{1,0:T(8,128)} %trial_source.1, f32[4,512,16]{2,1,0:T(8,128)} %get-tuple-element.4.coef_ref, f32[8,512]{1,0:T(8,128)} %get-tuple-element.5.edge_ref), custom_call_target="tpu_custom_call" | custom-call | tf_op jit(solution)/shard_map/trotter_step/pallas_call | solution.py:531
  83.7 0.0 copy-start
  83.7 4.7 %copy.11 = f32[2048,512]{1,0:T(8,128)} copy(f32[2048,512]{1,0:T(8,128)} %get-tuple-element.10) | data formatting | bytes 8388608
  88.5 0.0 copy-done
  88.5 1.0 %copy.12 = f32[512,512]{1,0:T(8,128)} copy(f32[512,512]{1,0:T(8,128)S(1)} %copy-done) | data formatting | bytes 2097152
Async XLA Ops:
  83.7 4.7 %copy-start = (f32[512,512]{1,0:T(8,128)S(1)}, f32[512,512]{1,0:T(8,128)}, u32[]{:S(2)}) copy-start(f32[512,512]{1,0:T(8,128)} %get-tuple-element.11) | copy-start | bytes 3145732
